TPU v7x, 256 devices: a whole 4x4x8 slice. The times are simulated.
256 devices in a mesh: cells: 64 (over z, x, core), cls: 4 (over y).
Axes of the slice: x: 4, y: 4, z: 8, core: 2. Of those that a mesh axis runs over, the one named last changes fastest.
Arguments:
- cotangent: float32 [4, 8192, 24, 128], P('cls', 'cells'), may hold values from -6 to 6
- departure: int32 [2, 8192], replicated, may hold values from 0 to 8191, as said below
- interp: bfloat16 [2, 8192, 128, 128], P(None, ('cells', 'cls')), may hold values from -0.5 to 0.5
- vertical_inv: float32 [4, 4, 24, 24], replicated, may hold values from -0.35 to 1.2
- regime: int32 [8192, 128], P('cells'), may hold values from 0 to 3
- bed_rate: float32 [4], replicated, may hold values from 0.3 to 1.5
Outputs:
- initial_grad: float32 [4, 8192, 24, 128], P('cls', 'cells')
Inputs may be any that keep to these rules, and one draw needn't show every extreme that they name: For a block of partition p (blocks p * 128 to p * 128 + 127), departure lies in partition p - d with 0 <= d <= min(4, p); in each step at most 32 blocks of one partition depart from one other partition; both bounds are reached.
All inputs are finite; a program needn't handle non-finite values.
Results may differ from a plain program's by a relative error of at most 0.0036.
Values may be sent and summed in bfloat16 or wider, within the bound.
A program may use at most 64 MiB of HBM per device.

v0:
```python
import jax
import jax.numpy as jnp
from jax import lax
from jax.sharding import PartitionSpec as P

NSET = 4
REACH = 4
STEPS = 2


def passed_along(array, axis, by):
    size = lax.axis_size(axis)
    pairs = [(i, i + by) for i in range(size) if 0 <= i + by < size]
    return lax.ppermute(array, axis, pairs)


def vertical(operators, regime, field):
    result = jnp.zeros(field.shape, jnp.float32)
    for regime_index in range(NSET):
        applied = jnp.einsum(
            "ml,bmi->bli", operators[regime_index], field, precision=lax.Precision.HIGHEST
        )
        result = result + jnp.where(regime[:, None, :] == regime_index, applied, jnp.float32(0.0))
    return result


def routing(routes, partition, blocks):
    offset = partition - routes // blocks
    target = routes % blocks
    one_hot = (offset[:, None] == jnp.arange(REACH + 1, dtype=jnp.int32)[None, :]).astype(jnp.int32)
    slot_rank = jnp.sum((jnp.cumsum(one_hot, axis=0) - 1) * one_hot, axis=1)
    return (offset, target, slot_rank)


def interpolate(adjoint, weight_shard):
    return jnp.einsum(
        "bli,bij->blj",
        adjoint,
        lax.all_gather(weight_shard, "cls", axis=0, tiled=True),
        preferred_element_type=jnp.float32,
    )


def upstream(products, routes_all, partition):
    blocks = products.shape[0]
    tail_shape = products.shape[1:]
    own_routes = lax.dynamic_slice_in_dim(routes_all, partition * blocks, blocks)
    offset, target, slot_rank = routing(own_routes, partition, blocks)
    segment_ids = offset * blocks + target
    offset_table = jax.ops.segment_sum(products, segment_ids, num_segments=(REACH + 1) * blocks)
    offset_table = offset_table.reshape((REACH + 1, blocks) + tail_shape)
    total = offset_table[0]
    for distance in range(1, REACH + 1):
        total = total + passed_along(offset_table[distance], "cells", -distance)
    return total


def local(cotangent, departure, interp, vertical_inv, regime, bed_rate):
    class_index = lax.axis_index("cls")
    partition = lax.axis_index("cells")
    layers = cotangent.shape[2]
    operators = lax.dynamic_index_in_dim(vertical_inv, class_index, 0, keepdims=False)
    bed_weight = lax.dynamic_index_in_dim(bed_rate, class_index, 0, keepdims=False)
    field = cotangent[0]
    for step_index in range(STEPS - 1, -1, -1):
        bottom = lax.psum(bed_weight * field[:, layers - 1, :], "cls")
        field = field.at[:, layers - 1, :].add(bottom)
        adjoint = vertical(operators, regime, field).astype(jnp.bfloat16)
        products = interpolate(adjoint, interp[step_index])
        field = upstream(products, departure[step_index], partition)
    return field[None]


def solution(mesh):
    placed = (
        P("cls", "cells", None, None),
        P(),
        P(None, ("cells", "cls"), None, None),
        P(),
        P("cells", None),
        P(),
    )
    return jax.shard_map(
        local, mesh=mesh, in_specs=placed, out_specs=P("cls", "cells", None, None), check_vma=False
    )
```

profile of v0, /device:TPU:100, one launch (start us, length us, event | category | flops | bytes accessed | tf_op | source)
XLA Modules:
  0.0 626.1 jit_solution(4000290849921096965)
XLA Ops:
  10.1 3.1 slice_bitcast_fusion
  13.5 44.5 %all-reduce.3.cloned.1.call-done = f32[128,128]{1,0:T(8,128)} async-done(((f32[128,128]{1,0:T(8,128)}), f32[128,128]{1,0:T(8,128)}) %all-reduce.3.cloned.1.call-update) | async-done | bytes 65552 | tf_op jit(solution)/shard_map/psum | solution.py:66
  66.7 44.5 %all-gather.5.cloned.1.call-done = bf16[1,128,128,128]{3,2,0,1:T(8,128)(2,1)} async-done(((bf16[1,32,128,128]{3,2,0,1:T(8,128)(2,1)}), bf16[1,128,128,128]{3,2,0,1:T(8,128)(2,1)}) %all-gather.5.cloned.1.call-update) | async-done | bytes 4194320 | tf_op jit(solution)/shard_map/all_gather | solution.py:39
  111.2 3.4 fusion.2
  114.6 3.6 broadcast.249.clone
  118.2 15.2 %scatter_fusion = f32[640,24,128]{2,1,0:T(8,128)} fusion(f32[640,24,128]{2,1,0:T(8,128)} %broadcast.249.clone, s32[128]{0:T(128)S(1)} %fusion.29, f32[128,24,128]{2,1,0:T(8,128)S(1)} %fusion.2), kind=kCustom, calls=%fused_computation | custom fusion | flops 393216 | bytes 4719104 | tf_op jit(solution)/shard_map/scatter-add | solution.py:50
  133.4 3.2 fusion.32
  141.0 4.3 collective-permute-start.2
  145.3 3.0 collective-permute-start.3
  148.3 22.9 %collective-permute-done = f32[128,24,128]{2,1,0:T(8,128)S(1)} collective-permute-done((f32[128,24,128]{2,1,0:T(8,128)S(1)}, f32[128,24,128]{2,1,0:T(8,128)S(1)}, u32[]{:S(2)}, u32[]{:S(2)}) %collective-permute-start) | collective-permute-done | bytes 1572896 | tf_op jit(solution)/shard_map/ppermute | solution.py:14
  171.2 35.6 %collective-permute-done.1 = f32[128,24,128]{2,1,0:T(8,128)S(1)} collective-permute-done((f32[128,24,128]{2,1,0:T(8,128)S(1)}, f32[128,24,128]{2,1,0:T(8,128)S(1)}, u32[]{:S(2)}, u32[]{:S(2)}) %collective-permute-start.1) | collective-permute-done | bytes 1572896 | tf_op jit(solution)/shard_map/ppermute | solution.py:14
  206.8 4.2 collective-permute-done.2
  211.0 102.3 %collective-permute-done.3 = f32[128,24,128]{2,1,0:T(8,128)S(1)} collective-permute-done((f32[128,24,128]{2,1,0:T(8,128)S(1)}, f32[128,24,128]{2,1,0:T(8,128)S(1)}, u32[]{:S(2)}, u32[]{:S(2)}) %collective-permute-start.3) | collective-permute-done | bytes 1572896 | tf_op jit(solution)/shard_map/ppermute | solution.py:14
  317.0 44.7 %all-reduce.5.cloned.1.call-done = f32[128,1,128]{2,1,0:T(1,128)} async-done(((f32[128,1,128]{2,1,0:T(1,128)}), f32[128,1,128]{2,1,0:T(1,128)}) %all-reduce.5.cloned.1.call-update) | async-done | bytes 65552 | tf_op jit(solution)/shard_map/psum | solution.py:66
  370.5 44.1 %all-gather.7.cloned.1.call-done = bf16[1,128,128,128]{3,2,0,1:T(8,128)(2,1)} async-done(((bf16[1,32,128,128]{3,2,0,1:T(8,128)(2,1)}), bf16[1,128,128,128]{3,2,0,1:T(8,128)(2,1)}) %all-gather.7.cloned.1.call-update) | async-done | bytes 4194320 | tf_op jit(solution)/shard_map/all_gather | solution.py:39
  414.6 3.4 fusion
  418.0 3.6 broadcast.249
  421.6 15.1 %scatter_fusion.1 = f32[640,24,128]{2,1,0:T(8,128)} fusion(f32[640,24,128]{2,1,0:T(8,128)} %broadcast.249, s32[128]{0:T(128)S(1)} %fusion.30, f32[128,24,128]{2,1,0:T(8,128)S(1)} %fusion), kind=kCustom, calls=%fused_computation.1 | custom fusion | flops 393216 | bytes 4719104 | tf_op jit(solution)/shard_map/scatter-add | solution.py:50
  436.7 3.2 fusion.31
  444.4 4.3 collective-permute-start.6
  451.4 23.2 %collective-permute-done.4 = f32[128,24,128]{2,1,0:T(8,128)S(1)} collective-permute-done((f32[128,24,128]{2,1,0:T(8,128)S(1)}, f32[128,24,128]{2,1,0:T(8,128)S(1)}, u32[]{:S(2)}, u32[]{:S(2)}) %collective-permute-start.4) | collective-permute-done | bytes 1572896 | tf_op jit(solution)/shard_map/ppermute | solution.py:14
  474.6 35.7 %collective-permute-done.5 = f32[128,24,128]{2,1,0:T(8,128)S(1)} collective-permute-done((f32[128,24,128]{2,1,0:T(8,128)S(1)}, f32[128,24,128]{2,1,0:T(8,128)S(1)}, u32[]{:S(2)}, u32[]{:S(2)}) %collective-permute-start.5) | collective-permute-done | bytes 1572896 | tf_op jit(solution)/shard_map/ppermute | solution.py:14
  510.3 4.1 collective-permute-done.6
  514.4 102.3 %collective-permute-done.7 = f32[128,24,128]{2,1,0:T(8,128)S(1)} collective-permute-done((f32[128,24,128]{2,1,0:T(8,128)S(1)}, f32[128,24,128]{2,1,0:T(8,128)S(1)}, u32[]{:S(2)}, u32[]{:S(2)}) %collective-permute-start.7) | collective-permute-done | bytes 1572896 | tf_op jit(solution)/shard_map/ppermute | solution.py:14
  (44 shorter events, 39.4 us)
Async XLA Ops:
  6.5 53.8 %copy-start = (f32[4,4,24,24]{3,2,1,0:T(8,128)S(1)}, f32[4,4,24,24]{3,2,1,0:T(8,128)}, u32[]{:S(2)}) copy-start(f32[4,4,24,24]{3,2,1,0:T(8,128)} %param.13) | copy-start | bytes 110596
  6.5 1.5 copy-start.3
  6.5 51.5 %all-reduce.3.cloned.1.call-start = ((), (), s32[]{:S(2)}) async-start(), calls=%async_computation | async-start | bytes 131072 | tf_op jit(solution)/shard_map/psum | solution.py:66
  10.1 3.3 copy-start.1
  10.1 3.4 copy-start.2
  10.1 101.2 %all-gather.5.cloned.1.call-start = ((), (), s32[]{:S(2)}) async-start(), calls=%async_computation.2 | async-start | bytes 5242880 | tf_op jit(solution)/shard_map/all_gather | solution.py:39
  13.3 348.4 %all-reduce.5.cloned.1.call-start = ((), (), s32[]{:S(2)}) async-start(), calls=%async_computation.1 | async-start | bytes 131072 | tf_op jit(solution)/shard_map/psum | solution.py:66
  136.6 34.6 %collective-permute-start = (f32[128,24,128]{2,1,0:T(8,128)S(1)}, f32[128,24,128]{2,1,0:T(8,128)S(1)}, u32[]{:S(2)}, u32[]{:S(2)}) collective-permute-start(f32[128,24,128]{2,1,0:T(8,128)S(1)} %get-tuple-element.33), channel_id=1, source_target_pairs={{4,0},{8,4},{12,8},{16,12},{20,16},{24,20},{28,24},{32,28},{36,32}... | collective-permute-start | bytes 4718600 | tf_op jit(solution)/shard_map/ppermute | solution.py:14
  138.5 68.3 %collective-permute-start.1 = (f32[128,24,128]{2,1,0:T(8,128)S(1)}, f32[128,24,128]{2,1,0:T(8,128)S(1)}, u32[]{:S(2)}, u32[]{:S(2)}) collective-permute-start(f32[128,24,128]{2,1,0:T(8,128)S(1)} %get-tuple-element.36), channel_id=1, source_target_pairs={{8,0},{12,4},{16,8},{20,12},{24,16},{28,20},{32,24},{36,28},{40,32... | collective-permute-start | bytes 4718600 | tf_op jit(solution)/shard_map/ppermute | solution.py:14
  141.0 70.0 %collective-permute-start.2 = (f32[128,24,128]{2,1,0:T(8,128)S(1)}, f32[128,24,128]{2,1,0:T(8,128)S(1)}, u32[]{:S(2)}, u32[]{:S(2)}) collective-permute-start(f32[128,24,128]{2,1,0:T(8,128)S(1)} %get-tuple-element.35), channel_id=1, source_target_pairs={{12,0},{16,4},{20,8},{24,12},{28,16},{32,20},{36,24},{40,28},{44,3... | collective-permute-start | bytes 4718600 | tf_op jit(solution)/shard_map/ppermute | solution.py:14
  145.3 168.0 %collective-permute-start.3 = (f32[128,24,128]{2,1,0:T(8,128)S(1)}, f32[128,24,128]{2,1,0:T(8,128)S(1)}, u32[]{:S(2)}, u32[]{:S(2)}) collective-permute-start(f32[128,24,128]{2,1,0:T(8,128)S(1)} %get-tuple-element.34), channel_id=1, source_target_pairs={{16,0},{20,4},{24,8},{28,12},{32,16},{36,20},{40,24},{44,28},{48,3... | collective-permute-start | bytes 4718600 | tf_op jit(solution)/shard_map/ppermute | solution.py:14
  316.4 98.2 %all-gather.7.cloned.1.call-start = ((), (), s32[]{:S(2)}) async-start(), calls=%async_computation.3 | async-start | bytes 5242880 | tf_op jit(solution)/shard_map/all_gather | solution.py:39
  440.0 34.7 %collective-permute-start.4 = (f32[128,24,128]{2,1,0:T(8,128)S(1)}, f32[128,24,128]{2,1,0:T(8,128)S(1)}, u32[]{:S(2)}, u32[]{:S(2)}) collective-permute-start(f32[128,24,128]{2,1,0:T(8,128)S(1)} %get-tuple-element.29), channel_id=1, source_target_pairs={{4,0},{8,4},{12,8},{16,12},{20,16},{24,20},{28,24},{32,28},{36,32}... | collective-permute-start | bytes 4718600 | tf_op jit(solution)/shard_map/ppermute | solution.py:14
  441.9 68.4 %collective-permute-start.5 = (f32[128,24,128]{2,1,0:T(8,128)S(1)}, f32[128,24,128]{2,1,0:T(8,128)S(1)}, u32[]{:S(2)}, u32[]{:S(2)}) collective-permute-start(f32[128,24,128]{2,1,0:T(8,128)S(1)} %get-tuple-element.32), channel_id=1, source_target_pairs={{8,0},{12,4},{16,8},{20,12},{24,16},{28,20},{32,24},{36,28},{40,32... | collective-permute-start | bytes 4718600 | tf_op jit(solution)/shard_map/ppermute | solution.py:14
  444.4 70.0 %collective-permute-start.6 = (f32[128,24,128]{2,1,0:T(8,128)S(1)}, f32[128,24,128]{2,1,0:T(8,128)S(1)}, u32[]{:S(2)}, u32[]{:S(2)}) collective-permute-start(f32[128,24,128]{2,1,0:T(8,128)S(1)} %get-tuple-element.31), channel_id=1, source_target_pairs={{12,0},{16,4},{20,8},{24,12},{28,16},{32,20},{36,24},{40,28},{44,3... | collective-permute-start | bytes 4718600 | tf_op jit(solution)/shard_map/ppermute | solution.py:14
  448.7 167.9 %collective-permute-start.7 = (f32[128,24,128]{2,1,0:T(8,128)S(1)}, f32[128,24,128]{2,1,0:T(8,128)S(1)}, u32[]{:S(2)}, u32[]{:S(2)}) collective-permute-start(f32[128,24,128]{2,1,0:T(8,128)S(1)} %get-tuple-element.30), channel_id=1, source_target_pairs={{16,0},{20,4},{24,8},{28,12},{32,16},{36,20},{40,24},{44,28},{48,3... | collective-permute-start | bytes 4718600 | tf_op jit(solution)/shard_map/ppermute | solution.py:14
Sparse Core Ops, SparseCore 0:
  10.2 47.7 all-reduce.2
  60.0 51.2 all-gather.4
  316.5 45.0 all-reduce.4
  363.3 51.2 all-gather.6
where the time goes:
time: 628 us; the launch traced here: 626 us
  waiting for transfers between devices  508 us (81%)
  other arithmetic  39.5 us (6%)
  starting transfers between devices  23.3 us (4%)
  local copies, waits for them, and re-layouts  21.9 us (3%)
  matrix products  19.6 us (3%)
  between operations  13.4 us (2%)
    ppermute x8, waiting for transfers between devices, passed_along(): return lax.ppermute(array, axis, pairs)  330 us
    psum x2, waiting for transfers between devices, local(): bottom = lax.psum(bed_weight * field[:, layers - 1, :], 'cls')  89.1 us
    all_gather x2, waiting for transfers between devices, interpolate(): lax.all_gather(weight_shard, 'cls', axis=0, tiled=True)  88.6 us
    scatter-add x2, other arithmetic, upstream(): jax.ops.segment_sum(products, segment_ids, num_segments=(REACH + 1) * blo...  30.3 us
    ppermute x8, starting transfers between devices, passed_along(): return lax.ppermute(array, axis, pairs)  23.1 us
    dot_general x8, matrix products, vertical(): jnp.einsum('ml,bmi->bli', operators[regime_index], field, precision=lax.P...  12.8 us
  transfers between devices with their start and end apart: 12, of which 12 were waited for; matrix products, arithmetic and copies ran while one was open for 3% of the time, Pallas kernels for 0%

commit v1 on v0

v1 whole, which is shorter than its diff:
```python
import jax
import jax.numpy as jnp
from jax import lax
from jax.experimental import pallas as pl
from jax.experimental.pallas import tpu as pltpu
from jax.sharding import PartitionSpec as P

CELLS = 64
CLS = 4
BLOCKS = 128
OWN = BLOCKS // CLS
LAYERS = 24
COLS = 128
NSET = 4
REACH = 4
CAP = 32
STEPS = 2
CHUNK = 8
CHUNKS = LAYERS // CHUNK
ORDER = (2, 1, 0)
ROWS = CHUNK * OWN
MESH = pl.DeviceIdType.MESH
F32 = jnp.float32
BF16 = jnp.bfloat16


def iota(shape, dim):
    return lax.broadcasted_iota(jnp.int32, shape, dim)


def ones_where(mask):
    return jnp.where(mask, F32(1.0), F32(0.0)).astype(BF16)


def nt_dot(a, b, **kw):
    return lax.dot_general(a, b, (((1,), (1,)), ((), ())), preferred_element_type=F32, **kw)


def build_operators(v_ref, lhs, cls):
    eye = jnp.where(iota((LAYERS, LAYERS), 0) == iota((LAYERS, LAYERS), 1), F32(1.0), F32(0.0))
    shape = (LAYERS, 4 * LAYERS)
    col, row = iota(shape, 1), iota(shape, 0)
    place_high = ones_where((col == row) | (col == row + LAYERS))
    place_low = ones_where((col == row + 2 * LAYERS) | (col == row + 3 * LAYERS))
    parts = []
    for r in range(NSET):
        turned = nt_dot(eye, v_ref[cls, r], precision=lax.Precision.HIGHEST)
        high = turned.astype(BF16)
        low = (turned - high.astype(F32)).astype(BF16)
        parts.append(
            jnp.dot(high, place_high, preferred_element_type=F32)
            + jnp.dot(low, place_low, preferred_element_type=F32)
        )
    lhs[...] = jnp.concatenate(parts, axis=0).astype(BF16)


def route(dep, s, q):
    row = dep[s : s + 1, pl.ds(pl.multiple_of(q * BLOCKS, BLOCKS), BLOCKS)]
    off = q - (row >> 7)
    tgt = row & (BLOCKS - 1)
    hot = jnp.where(iota((16, BLOCKS), 0) == off, F32(1.0), F32(0.0))
    tri = ones_where(iota((BLOCKS, BLOCKS), 0) < iota((BLOCKS, BLOCKS), 1))
    before = jnp.dot(hot.astype(BF16), tri, preferred_element_type=F32)
    rank = jnp.sum(before * hot, axis=0, keepdims=True).astype(jnp.int32)
    slot = jnp.where(off > 0, (off - 1) * CAP + rank, -1)
    return off, tgt, slot


def build_tables(dep, gather, total, s, me):
    square = (BLOCKS, BLOCKS)
    off, tgt, slot = route(dep, s, me)
    gather[s] = ones_where(iota(square, 0) == slot)
    total[s, :, :BLOCKS] = ones_where(iota(square, 0) == jnp.where(off == 0, tgt, -1))
    remote = jnp.zeros(square, F32)
    for d in range(1, REACH + 1):
        off, tgt, slot = route(dep, s, lax.rem(me + d, CELLS))
        aims = ones_where(iota(square, 0) == tgt)
        slots = ones_where(iota(square, 0) == jnp.where(off == d, slot, -1))
        remote = remote + nt_dot(aims, slots)
    total[s, :, BLOCKS:] = remote.astype(BF16)


def kernel(
    cot, dep, w, v_ref, reg, rate, out,
    adj, ra, sb, pr, xs, xr, fs, pf, bed_out, bed_in, bot, lhs, gather, total,
    bed_s, bed_r, a1_s, a1_r, a2_s, a2_r, x_s, x_r,
):
    me = lax.axis_index("cells")
    cls = lax.axis_index("cls")

    def over_y(k):
        return (me, lax.rem(cls + k, CLS))

    def along(d):
        return (lax.rem(me + d + CELLS, CELLS), cls)

    barrier = pltpu.get_barrier_semaphore()
    partners = [over_y(k) for k in range(1, CLS)]
    partners += [along(d) for d in range(-REACH, REACH + 1) if d != 0]
    for partner in partners:
        pl.semaphore_signal(barrier, inc=1, device_id=partner, device_id_type=MESH)

    pending = []

    def send(src, dst, ssem, rsem, device):
        copy = pltpu.make_async_remote_copy(
            src_ref=src, dst_ref=dst, send_sem=ssem, recv_sem=rsem,
            device_id=device, device_id_type=MESH,
        )
        copy.start()
        pending.append(copy)
        return copy

    build_operators(v_ref, lhs, cls)
    my_rate = rate[cls]

    def send_bed(s):
        return [
            send(bed_out.at[s], bed_in.at[s, k - 1], bed_s.at[s, k - 1], bed_r.at[s, k - 1], over_y(k))
            for k in range(1, CLS)
        ]

    def bottom_of(s, copies):
        for copy in copies:
            copy.wait_recv()
        return bed_out[s] + bed_in[s, 0] + bed_in[s, 1] + bed_in[s, 2]

    def vertical(s, load, dest):
        def body(n, carry):
            b = dest * OWN + 2 * n
            field = jnp.concatenate([load(b), load(b + 1)], axis=1)
            high = field.astype(BF16).astype(F32)
            low = field - high
            rhs = jnp.concatenate([high, low, high, low], axis=0).astype(BF16)
            res = jnp.dot(lhs[...], rhs, preferred_element_type=F32)
            r = jnp.concatenate([reg[pl.ds(b, 1), :], reg[pl.ds(b + 1, 1), :]], axis=1)
            picked = res[:LAYERS]
            for i in range(1, NSET):
                picked = jnp.where(r == i, res[i * LAYERS : (i + 1) * LAYERS], picked)
            at = pl.ds(pl.multiple_of(n * 16, 16), 16)
            for lc in range(CHUNKS):
                part = picked[lc * CHUNK : (lc + 1) * CHUNK]
                both = jnp.concatenate([part[:, :COLS], part[:, COLS:]], axis=0)
                adj[s, lc, dest, at, :] = both.astype(BF16)
            return carry

        lax.fori_loop(0, OWN // 2, body, 0)

    def interpolate(s, lc):
        def body(n, carry):
            at = pl.ds(pl.multiple_of(n * 16, 16), 16)
            tiles = [adj[s, lc, cls, at, :]] + [ra[s, lc, k, at, :] for k in range(CLS - 1)]
            weights = jnp.concatenate([w[s, 2 * n], w[s, 2 * n + 1]], axis=1)
            res = jnp.dot(jnp.concatenate(tiles, axis=0), weights, preferred_element_type=F32)
            for k in range(CLS):
                pf[k, pl.ds(2 * n, CHUNK, stride=OWN), :] = res[k * 16 : k * 16 + 8, :COLS]
                pf[k, pl.ds(2 * n + 1, CHUNK, stride=OWN), :] = res[k * 16 + 8 : k * 16 + 16, COLS:]
            return carry

        lax.fori_loop(0, OWN // 2, body, 0)
        for k in range(1, CLS):
            sb[s, lc, k - 1] = pf[k].astype(BF16)
        pr[s, lc, cls] = pf[0].astype(BF16)

    def plane_of(s, lc, at):
        return jnp.concatenate([pr[s, lc, y, at, :] for y in range(CLS)], axis=0)

    def pack(s, lc):
        def body(n, carry):
            ats = [pl.ds(pl.multiple_of((2 * n + i) * OWN, OWN), OWN) for i in range(2)]
            rhs = jnp.concatenate([plane_of(s, lc, at) for at in ats], axis=1)
            res = jnp.dot(gather[s], rhs, preferred_element_type=F32).astype(BF16)
            for d in range(REACH):
                for i, at in enumerate(ats):
                    xs[s, lc, d, at, :] = res[d * CAP : (d + 1) * CAP, i * COLS : (i + 1) * COLS]
            return carry

        lax.fori_loop(0, CHUNK // 2, body, 0)

    def accumulate(s, lc, dst):
        def body(n, carry):
            ats = [pl.ds(pl.multiple_of((2 * n + i) * OWN, OWN), OWN) for i in range(2)]
            cols = [
                jnp.concatenate(
                    [plane_of(s, lc, at)] + [xr[s, lc, d, at, :] for d in range(REACH)], axis=0
                )
                for at in ats
            ]
            res = jnp.dot(total[s], jnp.concatenate(cols, axis=1), preferred_element_type=F32)
            for i in range(2):
                at = pl.multiple_of((lc * CHUNK + 2 * n + i) * BLOCKS, BLOCKS)
                dst[pl.ds(at, BLOCKS), :] = res[:, i * COLS : (i + 1) * COLS]
            return carry

        lax.fori_loop(0, CHUNK // 2, body, 0)

    first = STEPS - 1
    bed_out[first] = my_rate * cot[:, LAYERS - 1, :]
    pl.semaphore_wait(barrier, len(partners))
    beds = send_bed(first)
    for s in range(STEPS):
        build_tables(dep, gather, total, s, me)

    for s in range(STEPS - 1, -1, -1):
        if s == first:
            bot[...] = bottom_of(s, beds)
            last = iota((LAYERS, COLS), 0) == LAYERS - 1

            def load(b):
                return cot[b] + jnp.where(last, bot[pl.ds(b, 1), :], F32(0.0))
        else:
            tail = pl.ds((LAYERS - 1) * BLOCKS, BLOCKS)
            fs[tail, :] = fs[tail, :] + bottom_of(s, beds)

            def load(b):
                return fs[pl.ds(b, LAYERS, stride=BLOCKS), :]

        a1 = {}

        def send_adjoint(lc, k):
            a1[lc, k] = send(
                adj.at[s, lc, lax.rem(cls + k, CLS)], ra.at[s, lc, k - 1],
                a1_s.at[s, lc, k - 1], a1_r.at[s, lc, k - 1], over_y(k),
            )

        for k in (2, 1, 3):
            vertical(s, load, lax.rem(cls + k, CLS))
            send_adjoint(ORDER[0], k)
        for lc in ORDER[1:]:
            for k in (2, 1, 3):
                send_adjoint(lc, k)
        vertical(s, load, cls)

        a2 = {}
        for lc in ORDER:
            for k in range(1, CLS):
                a1[lc, k].wait_recv()
            interpolate(s, lc)
            for k in range(1, CLS):
                a2[lc, k] = send(
                    sb.at[s, lc, k - 1], pr.at[s, lc, cls],
                    a2_s.at[s, lc, k - 1], a2_r.at[s, lc, k - 1], over_y(CLS - k),
                )
        x = {}
        for lc in ORDER:
            for k in range(1, CLS):
                a2[lc, k].wait_recv()
            pack(s, lc)
            for d in range(REACH, 0, -1):
                x[lc, d] = send(
                    xs.at[s, lc, d - 1], xr.at[s, lc, d - 1],
                    x_s.at[s, lc, d - 1], x_r.at[s, lc, d - 1], along(-d),
                )
        for lc in ORDER:
            for d in range(1, REACH + 1):
                x[lc, d].wait_recv()
            accumulate(s, lc, fs if s > 0 else out)
            if s > 0 and lc == ORDER[0]:
                bed_out[s - 1] = my_rate * fs[pl.ds((LAYERS - 1) * BLOCKS, BLOCKS), :]
                beds = send_bed(s - 1)

    for copy in pending:
        copy.wait_send()


def local(cotangent, departure, interp, vertical_inv, regime, bed_rate):
    vmem = pl.BlockSpec(memory_space=pltpu.VMEM)
    dma = pltpu.SemaphoreType.DMA
    result = pl.pallas_call(
        kernel,
        out_shape=jax.ShapeDtypeStruct((LAYERS * BLOCKS, COLS), F32),
        in_specs=[vmem] * 5 + [pl.BlockSpec(memory_space=pltpu.SMEM)],
        out_specs=vmem,
        scratch_shapes=[
            pltpu.VMEM((STEPS, CHUNKS, CLS, ROWS, COLS), BF16),
            pltpu.VMEM((STEPS, CHUNKS, CLS - 1, ROWS, COLS), BF16),
            pltpu.VMEM((STEPS, CHUNKS, CLS - 1, ROWS, COLS), BF16),
            pltpu.VMEM((STEPS, CHUNKS, CLS, ROWS, COLS), BF16),
            pltpu.VMEM((STEPS, CHUNKS, REACH, ROWS, COLS), BF16),
            pltpu.VMEM((STEPS, CHUNKS, REACH, ROWS, COLS), BF16),
            pltpu.VMEM((LAYERS * BLOCKS, COLS), F32),
            pltpu.VMEM((CLS, ROWS, COLS), F32),
            pltpu.VMEM((STEPS, BLOCKS, COLS), F32),
            pltpu.VMEM((STEPS, CLS - 1, BLOCKS, COLS), F32),
            pltpu.VMEM((BLOCKS, COLS), F32),
            pltpu.VMEM((NSET * LAYERS, 4 * LAYERS), BF16),
            pltpu.VMEM((STEPS, BLOCKS, BLOCKS), BF16),
            pltpu.VMEM((STEPS, BLOCKS, 2 * BLOCKS), BF16),
            dma((STEPS, CLS - 1)),
            dma((STEPS, CLS - 1)),
            dma((STEPS, CHUNKS, CLS - 1)),
            dma((STEPS, CHUNKS, CLS - 1)),
            dma((STEPS, CHUNKS, CLS - 1)),
            dma((STEPS, CHUNKS, CLS - 1)),
            dma((STEPS, CHUNKS, REACH)),
            dma((STEPS, CHUNKS, REACH)),
        ],
        compiler_params=pltpu.CompilerParams(
            collective_id=0, has_side_effects=True, vmem_limit_bytes=40 * 1024 * 1024
        ),
        cost_estimate=pl.CostEstimate(flops=2_000_000_000, bytes_accessed=6_000_000, transcendentals=0),
    )(cotangent[0], departure, interp, vertical_inv, regime, bed_rate)
    return jnp.swapaxes(result.reshape(LAYERS, BLOCKS, COLS), 0, 1)[None]


def solution(mesh):
    placed = (
        P("cls", "cells", None, None),
        P(),
        P(None, ("cells", "cls"), None, None),
        P(),
        P("cells", None),
        P(),
    )
    return jax.shard_map(
        local, mesh=mesh, in_specs=placed, out_specs=P("cls", "cells", None, None), check_vma=False
    )
```

time: 628 us -> 98.1 us (0.16)
  the two profiles are of different devices: /device:TPU:100 before, /device:TPU:71 now
where the time goes in v1:
time: 98.1 us; the launch traced here: 97 us
  Pallas kernels  88.6 us (90%)
  local copies, waits for them, and re-layouts  8.31 us (8%)
    pallas_call x1, Pallas kernels, local(): pl.pallas_call(kernel, out_shape=jax.ShapeDtypeStruct((LAYERS * BLOCKS, C...  88.6 us
    unnamed x12, local copies, waits for them, and re-layouts  6.26 us
    reshape x1, local copies, waits for them, and re-layouts, local(): return jnp.swapaxes(result.reshape(LAYERS, BLOCKS, COLS), 0, 1)[None]  2.06 us

profile of v1, /device:TPU:71, one launch (start us, length us, event | category | flops | bytes accessed | tf_op | source)
XLA Modules:
  0.0 97.0 jit_solution(14705213709181909507)
XLA Ops:
  0.0 0.0 copy-start
  0.0 1.6 %copy-done = bf16[2,32,128,128]{3,2,1,0:T(8,128)(2,1)S(1)} copy-done((bf16[2,32,128,128]{3,2,1,0:T(8,128)(2,1)S(1)}, bf16[2,32,128,128]{3,2,1,0:T(8,128)(2,1)}, u32[]{:S(2)}) %copy-start) | copy-done | bytes 2097176
  1.6 0.0 copy-start.1
  1.6 1.4 %copy-done.1 = f32[1,128,24,128]{3,2,1,0:T(8,128)S(1)} copy-done((f32[1,128,24,128]{3,2,1,0:T(8,128)S(1)}, f32[1,128,24,128]{3,2,1,0:T(8,128)}, u32[]{:S(2)}) %copy-start.1) | copy-done | bytes 1572888
  3.0 0.0 copy-start.2
  3.0 0.9 copy-done.2
  3.9 0.0 copy-start.3
  3.9 0.8 copy-done.3
  4.8 0.0 copy-start.4
  4.8 0.8 copy-done.4
  5.6 0.0 copy-start.5
  5.6 0.7 copy-done.5
  6.3 88.6 %shard_map.64 = f32[3072,128]{1,0:T(8,128)S(1)} custom-call(f32[128,24,128]{2,1,0:T(8,128)S(1)} %bitcast.8, s32[2,8192]{1,0:T(2,128)S(1)} %copy-done.3, bf16[2,32,128,128]{3,2,1,0:T(8,128)(2,1)S(1)} %copy-done, f32[4,4,24,24]{3,2,1,0:T(8,128)S(1)} %copy-done.2, s32[128,128]{1,0:T(8,128)S(1)} %copy-done.4, f32[4]{0:T(128)S(1)} %copy-done.5), custom_call_target="tpu_custom_call" | custom-call | flops 2000000000 | bytes 6000000 | tf_op jit(solution)/shard_map/pallas_call | solution.py:269
  94.9 2.1 %copy.9 = f32[24,128,128]{2,0,1:T(8,128)} copy(f32[24,128,128]{2,1,0:T(8,128)S(1)} %bitcast.7) | data formatting | bytes 3145728 | tf_op jit(solution)/shard_map/reshape | solution.py:303
Async XLA Ops:
  0.0 1.6 %copy-start = (bf16[2,32,128,128]{3,2,1,0:T(8,128)(2,1)S(1)}, bf16[2,32,128,128]{3,2,1,0:T(8,128)(2,1)}, u32[]{:S(2)}) copy-start(bf16[2,32,128,128]{3,2,1,0:T(8,128)(2,1)} %w.1) | copy-start | bytes 6291460
  1.6 1.4 %copy-start.1 = (f32[1,128,24,128]{3,2,1,0:T(8,128)S(1)}, f32[1,128,24,128]{3,2,1,0:T(8,128)}, u32[]{:S(2)}) copy-start(f32[1,128,24,128]{3,2,1,0:T(8,128)} %param.6) | copy-start | bytes 4718596
  3.0 0.9 copy-start.2
  3.9 0.8 copy-start.3
  4.8 0.8 copy-start.4
  5.6 0.7 copy-start.5

commit v2 on v1

v2 whole, which is shorter than its diff:
```python
import jax
import jax.numpy as jnp
from jax import lax
from jax.experimental import pallas as pl
from jax.experimental.pallas import tpu as pltpu
from jax.sharding import PartitionSpec as P

CELLS = 64
CLS = 4
BLOCKS = 128
OWN = BLOCKS // CLS
LAYERS = 24
COLS = 128
NSET = 4
REACH = 4
CAP = 32
STEPS = 2
CHUNK = 8
CHUNKS = LAYERS // CHUNK
ORDER = (2, 1, 0)
DESTS = (2, 1, 3, 0)
X_CHIPS = 4
ROWS = CHUNK * OWN
HALF = ROWS // 2
DIRECT = ((0, 0), (0, 1))
V_PAIRS = 16
I_PAIRS = 16
MESH = pl.DeviceIdType.MESH
F32 = jnp.float32
BF16 = jnp.bfloat16


def iota(shape, dim):
    return lax.broadcasted_iota(jnp.int32, shape, dim)


def ones_where(mask):
    return jnp.where(mask, F32(1.0), F32(0.0)).astype(BF16)


def nt_dot(a, b, **kw):
    return lax.dot_general(a, b, (((1,), (1,)), ((), ())), preferred_element_type=F32, **kw)


def build_operators(v_ref, lhs, cls):
    eye = jnp.where(iota((LAYERS, LAYERS), 0) == iota((LAYERS, LAYERS), 1), F32(1.0), F32(0.0))
    shape = (LAYERS, 4 * LAYERS)
    col, row = iota(shape, 1), iota(shape, 0)
    place_high = ones_where((col == row) | (col == row + LAYERS))
    place_low = ones_where((col == row + 2 * LAYERS) | (col == row + 3 * LAYERS))
    parts = []
    for r in range(NSET):
        turned = nt_dot(eye, v_ref[cls, r], precision=lax.Precision.HIGHEST)
        high = turned.astype(BF16)
        low = (turned - high.astype(F32)).astype(BF16)
        parts.append(
            jnp.dot(high, place_high, preferred_element_type=F32)
            + jnp.dot(low, place_low, preferred_element_type=F32)
        )
    lhs[...] = jnp.concatenate(parts, axis=0).astype(BF16)


def route(dep, s, q):
    row = dep[s : s + 1, pl.ds(pl.multiple_of(q * BLOCKS, BLOCKS), BLOCKS)]
    off = q - (row >> 7)
    tgt = row & (BLOCKS - 1)
    hot = jnp.where(iota((16, BLOCKS), 0) == off, F32(1.0), F32(0.0))
    tri = ones_where(iota((BLOCKS, BLOCKS), 0) < iota((BLOCKS, BLOCKS), 1))
    before = jnp.dot(hot.astype(BF16), tri, preferred_element_type=F32)
    rank = jnp.sum(before * hot, axis=0, keepdims=True).astype(jnp.int32)
    slot = jnp.where(off > 0, (off - 1) * CAP + rank, -1)
    return off, tgt, slot


def build_tables(dep, gather, total, s, me):
    square = (BLOCKS, BLOCKS)
    off, tgt, slot = route(dep, s, me)
    gather[s] = ones_where(iota(square, 0) == slot)
    total[s, :, :BLOCKS] = ones_where(iota(square, 0) == jnp.where(off == 0, tgt, -1))
    remote = jnp.zeros(square, F32)
    for d in range(1, REACH + 1):
        off, tgt, slot = route(dep, s, lax.rem(me + d, CELLS))
        aims = ones_where(iota(square, 0) == tgt)
        slots = ones_where(iota(square, 0) == jnp.where(off == d, slot, -1))
        remote = remote + nt_dot(aims, slots)
    total[s, :, BLOCKS:] = remote.astype(BF16)


def x_shift(p, by):
    x = (p // 2) % X_CHIPS
    return p + 2 * ((x + by + X_CHIPS) % X_CHIPS - x)


def kernel(
    cot_hbm, dep_hbm, w_hbm, v_hbm, reg_hbm, rate, out,
    cot, dep, w, v_ref, reg, adj, ra, sb, pr, xs, xr, rl, fs, pf, bed_out, bed_in, bot, lhs,
    gather, total, load_sem, out_sem, bed_s, bed_r, a1_s, a1_r, a2_s, a2_r, x_s, x_r, rl_s, rl_r,
):
    me = lax.axis_index("cells")
    cls = lax.axis_index("cls")

    split = LAYERS - CHUNK
    arrays = [
        (cot_hbm.at[:, split:, :], cot.at[:, split:, :]),
        (cot_hbm.at[:, :split, :], cot.at[:, :split, :]),
        (v_hbm, v_ref),
        (reg_hbm, reg),
        (dep_hbm, dep),
        (w_hbm, w),
    ]
    loads = [
        pltpu.make_async_copy(src, dst, load_sem.at[i]) for i, (src, dst) in enumerate(arrays)
    ]
    for copy in loads:
        copy.start()

    def over_y(k):
        return (me, lax.rem(cls + k, CLS))

    def along(d):
        return (lax.rem(me + d + CELLS, CELLS), cls)

    relay = (x_shift(me, 1), cls)
    relay_of = (x_shift(me, -1), cls)
    final = (lax.rem(x_shift(me, -1) - REACH + CELLS, CELLS), cls)
    final_of = (x_shift(lax.rem(me + REACH, CELLS), 1), cls)

    barrier = pltpu.get_barrier_semaphore()
    partners = [over_y(k) for k in range(1, CLS)]
    partners += [along(d) for d in range(-REACH, REACH + 1) if d != 0]
    partners += [relay, relay_of, final, final_of]
    for partner in partners:
        pl.semaphore_signal(barrier, inc=1, device_id=partner, device_id_type=MESH)

    pending = []

    def send(src, dst, ssem, rsem, device):
        copy = pltpu.make_async_remote_copy(
            src_ref=src, dst_ref=dst, send_sem=ssem, recv_sem=rsem,
            device_id=device, device_id_type=MESH,
        )
        copy.start()
        pending.append(copy)
        return copy

    my_rate = rate[cls]

    def own_rows(dest):
        return pl.ds(pl.multiple_of(dest * OWN, OWN), OWN)

    def send_bed(s):
        copies = {}
        for i in DESTS:
            for k in range(1, CLS):
                at = own_rows(lax.rem(cls + k + i, CLS))
                copies[i, k] = send(
                    bed_out.at[s, at], bed_in.at[s, k - 1, at],
                    bed_s.at[s, i, k - 1], bed_r.at[s, i, k - 1], over_y(k),
                )
        return copies

    def bottom_of(s, copies, i, dest):
        at = own_rows(dest)
        for k in range(1, CLS):
            copies[i, k].wait_recv()
        return bed_out[s, at] + bed_in[s, 0, at] + bed_in[s, 1, at] + bed_in[s, 2, at]

    def vertical(s, load, dest):
        def operands(b):
            field = jnp.concatenate([load(b), load(b + 1)], axis=1)
            high = field.astype(BF16).astype(F32)
            low = field - high
            return jnp.concatenate([high, low, high, low], axis=0).astype(BF16)

        def pick(b, res):
            r = jnp.concatenate([reg[pl.ds(b, 1), :], reg[pl.ds(b + 1, 1), :]], axis=1)
            picked = res[:LAYERS]
            for i in range(1, NSET):
                picked = jnp.where(r == i, res[i * LAYERS : (i + 1) * LAYERS], picked)
            return picked

        def body(g, carry):
            ns = [g * V_PAIRS + i for i in range(V_PAIRS)]
            bs = [dest * OWN + 2 * n for n in ns]
            rhs = [operands(b) for b in bs]
            res = [jnp.dot(lhs[...], x, preferred_element_type=F32) for x in rhs]
            for n, b, x in zip(ns, bs, res):
                picked = pick(b, x)
                at = pl.ds(pl.multiple_of(n * 16, 16), 16)
                for lc in range(CHUNKS):
                    part = picked[lc * CHUNK : (lc + 1) * CHUNK]
                    both = jnp.concatenate([part[:, :COLS], part[:, COLS:]], axis=0)
                    adj[s, lc, dest, at, :] = both.astype(BF16)
            return carry

        lax.fori_loop(0, OWN // 2 // V_PAIRS, body, 0)

    def interpolate(s, lc):
        def body(g, carry):
            ns = [g * I_PAIRS + i for i in range(I_PAIRS)]
            res = []
            for n in ns:
                at = pl.ds(pl.multiple_of(n * 16, 16), 16)
                tiles = [adj[s, lc, cls, at, :]] + [ra[s, lc, k, at, :] for k in range(CLS - 1)]
                weights = jnp.concatenate([w[s, 2 * n], w[s, 2 * n + 1]], axis=1)
                res.append(
                    jnp.dot(jnp.concatenate(tiles, axis=0), weights, preferred_element_type=F32)
                )
            for n, x in zip(ns, res):
                for k in range(CLS):
                    pf[k, pl.ds(2 * n, CHUNK, stride=OWN), :] = x[k * 16 : k * 16 + 8, :COLS]
                    pf[k, pl.ds(2 * n + 1, CHUNK, stride=OWN), :] = x[k * 16 + 8 : k * 16 + 16, COLS:]
            return carry

        lax.fori_loop(0, OWN // 2 // I_PAIRS, body, 0)
        for k in range(1, CLS):
            sb[s, lc, k - 1] = pf[k].astype(BF16)
        pr[s, lc, cls] = pf[0].astype(BF16)

    def plane_of(s, lc, at):
        return jnp.concatenate([pr[s, lc, y, at, :] for y in range(CLS)], axis=0)

    def pairs(lc, h):
        for n in range(CHUNK // 4):
            at = h * CHUNK // 2 + 2 * n
            yield [pl.ds((at + i) * OWN, OWN) for i in range(2)], lc * CHUNK + at

    def pack(s, lc, h):
        for ats, _ in pairs(lc, h):
            rhs = jnp.concatenate([plane_of(s, lc, at) for at in ats], axis=1)
            res = jnp.dot(gather[s], rhs, preferred_element_type=F32).astype(BF16)
            for d in range(REACH):
                for i, at in enumerate(ats):
                    xs[s, lc, d, at, :] = res[d * CAP : (d + 1) * CAP, i * COLS : (i + 1) * COLS]

    def accumulate(s, lc, h, dst):
        for ats, layer in pairs(lc, h):
            cols = [
                jnp.concatenate(
                    [plane_of(s, lc, at)] + [xr[s, lc, d, at, :] for d in range(REACH)], axis=0
                )
                for at in ats
            ]
            res = jnp.dot(total[s], jnp.concatenate(cols, axis=1), preferred_element_type=F32)
            for i in range(2):
                dst[pl.ds((layer + i) * BLOCKS, BLOCKS), :] = res[:, i * COLS : (i + 1) * COLS]

    first = STEPS - 1
    tail = (LAYERS - 1) * BLOCKS
    loads[0].wait()
    bed_out[first] = my_rate * cot[:, LAYERS - 1, :]
    pl.semaphore_wait(barrier, len(partners))
    beds = send_bed(first)
    for copy in loads[1:]:
        copy.wait()
    build_operators(v_ref, lhs, cls)

    stores = []
    for s in range(STEPS - 1, -1, -1):
        if s == first:
            last = iota((LAYERS, COLS), 0) == LAYERS - 1

            def add_bottom(i, dest):
                bot[own_rows(dest)] = bottom_of(s, beds, i, dest)

            def load(b):
                return cot[b] + jnp.where(last, bot[pl.ds(b, 1), :], F32(0.0))
        else:

            def add_bottom(i, dest):
                at = pl.ds(pl.multiple_of(tail + dest * OWN, OWN), OWN)
                fs[at, :] = fs[at, :] + bottom_of(s, beds, i, dest)

            def load(b):
                return fs[pl.ds(b, LAYERS, stride=BLOCKS), :]

        a1, a2, x, via = {}, {}, {}, {}

        def send_adjoint(lc, k):
            a1[lc, k] = send(
                adj.at[s, lc, lax.rem(cls + k, CLS)], ra.at[s, lc, k - 1],
                a1_s.at[s, lc, k - 1], a1_r.at[s, lc, k - 1], over_y(k),
            )

        def exchange(lc):
            for k in range(1, CLS):
                a1[lc, k].wait_recv()
            interpolate(s, lc)

        def rows(h):
            return pl.ds(h * HALF, HALF)

        def send_back(lc, h):
            for k in (2, 1, 3):
                a2[lc, h, k] = send(
                    sb.at[s, lc, k - 1, rows(h)], pr.at[s, lc, cls, rows(h)],
                    a2_s.at[s, lc, h, k - 1], a2_r.at[s, lc, h, k - 1], over_y(CLS - k),
                )

        def send_along(lc, h, d, src, device):
            x[lc, h, d] = send(
                src, xr.at[s, lc, d - 1, rows(h)],
                x_s.at[s, lc, h, d - 1], x_r.at[s, lc, h, d - 1], device,
            )

        def depart(lc, h):
            for k in range(1, CLS):
                a2[lc, h, k].wait_recv()
            pack(s, lc, h)
            far = xs.at[s, lc, REACH - 1, rows(h)]
            if (lc, h) in DIRECT:
                send_along(lc, h, REACH, far, along(-REACH))
            else:
                via[lc, h] = send(
                    far, rl.at[s, lc, rows(h)], rl_s.at[s, lc, h], rl_r.at[s, lc, h], relay
                )
            for d in range(REACH - 1, 0, -1):
                send_along(lc, h, d, xs.at[s, lc, d - 1, rows(h)], along(-d))

        def forward(lc, h):
            if (lc, h) not in DIRECT:
                via[lc, h].wait_recv()
                send_along(lc, h, REACH, rl.at[s, lc, rows(h)], final)

        def arrive(lc, h):
            for d in range(1, REACH + 1):
                x[lc, h, d].wait_recv()
            accumulate(s, lc, h, fs)
            if s == 0:
                size = HALF // OWN * BLOCKS
                at = pl.ds((lc * 2 + h) * size, size)
                copy = pltpu.make_async_copy(fs.at[at, :], out.at[at, :], out_sem.at[lc, h])
                copy.start()
                stores.append(copy)

        c0, c1, c2 = ORDER
        for i in DESTS:
            dest = lax.rem(cls + i, CLS)
            add_bottom(i, dest)
            vertical(s, load, dest)
            if i:
                send_adjoint(c0, i)
        for k in DESTS[:-1]:
            send_adjoint(c1, k)
        if s == first:
            for each in range(STEPS - 1, -1, -1):
                build_tables(dep, gather, total, each, me)
        exchange(c0)
        send_back(c0, 0)
        send_back(c0, 1)
        exchange(c1)
        send_back(c1, 0)
        for k in DESTS[:-1]:
            send_adjoint(c2, k)
        send_back(c1, 1)
        depart(c0, 0)
        depart(c0, 1)
        forward(c0, 0)
        depart(c1, 0)
        forward(c0, 1)
        exchange(c2)
        send_back(c2, 0)
        send_back(c2, 1)
        depart(c1, 1)
        forward(c1, 0)
        arrive(c0, 0)
        arrive(c0, 1)
        depart(c2, 0)
        forward(c1, 1)
        depart(c2, 1)
        if s > 0:
            bed_out[s - 1] = my_rate * fs[pl.ds(tail, BLOCKS), :]
            beds = send_bed(s - 1)
        forward(c2, 0)
        arrive(c1, 0)
        arrive(c1, 1)
        forward(c2, 1)
        arrive(c2, 0)
        arrive(c2, 1)

    for copy in pending:
        copy.wait_send()
    for copy in stores:
        copy.wait()


def local(cotangent, departure, interp, vertical_inv, regime, bed_rate):
    hbm = pl.BlockSpec(memory_space=pltpu.HBM)
    dma = pltpu.SemaphoreType.DMA
    result = pl.pallas_call(
        kernel,
        out_shape=jax.ShapeDtypeStruct((LAYERS * BLOCKS, COLS), F32),
        in_specs=[hbm] * 5 + [pl.BlockSpec(memory_space=pltpu.SMEM)],
        out_specs=hbm,
        scratch_shapes=[
            pltpu.VMEM((BLOCKS, LAYERS, COLS), F32),
            pltpu.VMEM((STEPS, CELLS * BLOCKS), jnp.int32),
            pltpu.VMEM((STEPS, OWN, COLS, COLS), BF16),
            pltpu.VMEM((CLS, NSET, LAYERS, LAYERS), F32),
            pltpu.VMEM((BLOCKS, COLS), jnp.int32),
            pltpu.VMEM((STEPS, CHUNKS, CLS, ROWS, COLS), BF16),
            pltpu.VMEM((STEPS, CHUNKS, CLS - 1, ROWS, COLS), BF16),
            pltpu.VMEM((STEPS, CHUNKS, CLS - 1, ROWS, COLS), BF16),
            pltpu.VMEM((STEPS, CHUNKS, CLS, ROWS, COLS), BF16),
            pltpu.VMEM((STEPS, CHUNKS, REACH, ROWS, COLS), BF16),
            pltpu.VMEM((STEPS, CHUNKS, REACH, ROWS, COLS), BF16),
            pltpu.VMEM((STEPS, CHUNKS, ROWS, COLS), BF16),
            pltpu.VMEM((LAYERS * BLOCKS, COLS), F32),
            pltpu.VMEM((CLS, ROWS, COLS), F32),
            pltpu.VMEM((STEPS, BLOCKS, COLS), F32),
            pltpu.VMEM((STEPS, CLS - 1, BLOCKS, COLS), F32),
            pltpu.VMEM((BLOCKS, COLS), F32),
            pltpu.VMEM((NSET * LAYERS, 4 * LAYERS), BF16),
            pltpu.VMEM((STEPS, BLOCKS, BLOCKS), BF16),
            pltpu.VMEM((STEPS, BLOCKS, 2 * BLOCKS), BF16),
            dma((6,)),
            dma((CHUNKS, 2)),
        ]
        + [dma((STEPS, CLS, CLS - 1))] * 2
        + [dma((STEPS, CHUNKS, CLS - 1))] * 2
        + [dma((STEPS, CHUNKS, 2, CLS - 1))] * 2
        + [dma((STEPS, CHUNKS, 2, REACH))] * 2
        + [dma((STEPS, CHUNKS, 2))] * 2,
        compiler_params=pltpu.CompilerParams(
            collective_id=0, has_side_effects=True, vmem_limit_bytes=56 * 1024 * 1024
        ),
        cost_estimate=pl.CostEstimate(flops=2_000_000_000, bytes_accessed=6_000_000, transcendentals=0),
    )(cotangent[0], departure, interp, vertical_inv, regime, bed_rate)
    return jnp.swapaxes(result.reshape(LAYERS, BLOCKS, COLS), 0, 1)[None]


def solution(mesh):
    placed = (
        P("cls", "cells", None, None),
        P(),
        P(None, ("cells", "cls"), None, None),
        P(),
        P("cells", None),
        P(),
    )
    return jax.shard_map(
        local, mesh=mesh, in_specs=placed, out_specs=P("cls", "cells", None, None), check_vma=False
    )
```

time: 98.1 us -> 75.4 us (0.77)
  Pallas kernels: 88.6 us -> 71 us
  local copies, waits for them, and re-layouts: 8.31 us -> 3.46 us
    pallas_call x1, Pallas kernels: 88.6 us -> 71 us  [local(): pl.pallas_call(kernel, out_shape=jax.ShapeDtypeStruct((LAYERS * BLOCKS, C...]
    unnamed x12 -> x0, local copies, waits for them, and re-layouts: 6.26 us -> none
    reshape x1, local copies, waits for them, and re-layouts: 2.06 us -> 3.46 us  [local(): return jnp.swapaxes(result.reshape(LAYERS, BLOCKS, COLS), 0, 1)[None]]
where the time goes in v2:
time: 75.4 us; the launch traced here: 74.5 us
  Pallas kernels  71 us (94%)
  local copies, waits for them, and re-layouts  3.46 us (5%)
    pallas_call x1, Pallas kernels, local(): pl.pallas_call(kernel, out_shape=jax.ShapeDtypeStruct((LAYERS * BLOCKS, C...  71 us
    reshape x1, local copies, waits for them, and re-layouts, local(): return jnp.swapaxes(result.reshape(LAYERS, BLOCKS, COLS), 0, 1)[None]  3.46 us

profile of v2, /device:TPU:71, one launch (start us, length us, event | category | flops | bytes accessed | tf_op | source)
XLA Modules:
  0.0 74.5 jit_solution(2141540739823995887)
XLA Ops:
  0.0 71.0 %shard_map.64 = f32[3072,128]{1,0:T(8,128)} custom-call(f32[128,24,128]{2,1,0:T(8,128)} %bitcast.8, s32[2,8192]{1,0:T(2,128)} %dep_hbm.1, bf16[2,32,128,128]{3,2,1,0:T(8,128)(2,1)} %w_hbm.1, f32[4,4,24,24]{3,2,1,0:T(8,128)} %v_hbm.1, s32[128,128]{1,0:T(8,128)} %reg_hbm.1, f32[4]{0:T(128)} %rate.1), custom_call_target="tpu_custom_call" | custom-call | flops 2000000000 | bytes 6000000 | tf_op jit(solution)/shard_map/pallas_call | solution.py:390
  71.0 3.5 %copy.9 = f32[24,128,128]{2,0,1:T(8,128)} copy(f32[24,128,128]{2,1,0:T(8,128)} %bitcast.7) | data formatting | bytes 3145728 | tf_op jit(solution)/shard_map/reshape | solution.py:429

commit v3 on v2

--- a/solution.py
+++ b/solution.py
@@ -19,10 +19,9 @@
 CHUNKS = LAYERS // CHUNK
 ORDER = (2, 1, 0)
 DESTS = (2, 1, 3, 0)
-X_CHIPS = 4
+PIECES = 4
 ROWS = CHUNK * OWN
 HALF = ROWS // 2
-DIRECT = ((0, 0), (0, 1))
 V_PAIRS = 16
 I_PAIRS = 16
 MESH = pl.DeviceIdType.MESH
@@ -86,15 +85,10 @@
     total[s, :, BLOCKS:] = remote.astype(BF16)
 
 
-def x_shift(p, by):
-    x = (p // 2) % X_CHIPS
-    return p + 2 * ((x + by + X_CHIPS) % X_CHIPS - x)
-
-
 def kernel(
     cot_hbm, dep_hbm, w_hbm, v_hbm, reg_hbm, rate, out,
-    cot, dep, w, v_ref, reg, adj, ra, sb, pr, xs, xr, rl, fs, pf, bed_out, bed_in, bot, lhs,
-    gather, total, load_sem, out_sem, bed_s, bed_r, a1_s, a1_r, a2_s, a2_r, x_s, x_r, rl_s, rl_r,
+    cot, dep, w, v_ref, reg, adj, ra, sb, pr, xs, xr, fs, ob, pf, bed_out, bed_in, bot, lhs,
+    gather, total, load_sem, out_sem, bed_s, bed_r, a1_s, a1_r, a2_s, a2_r, x_s, x_r,
 ):
     me = lax.axis_index("cells")
     cls = lax.axis_index("cls")
@@ -120,15 +114,9 @@
     def along(d):
         return (lax.rem(me + d + CELLS, CELLS), cls)
 
-    relay = (x_shift(me, 1), cls)
-    relay_of = (x_shift(me, -1), cls)
-    final = (lax.rem(x_shift(me, -1) - REACH + CELLS, CELLS), cls)
-    final_of = (x_shift(lax.rem(me + REACH, CELLS), 1), cls)
-
     barrier = pltpu.get_barrier_semaphore()
     partners = [over_y(k) for k in range(1, CLS)]
     partners += [along(d) for d in range(-REACH, REACH + 1) if d != 0]
-    partners += [relay, relay_of, final, final_of]
     for partner in partners:
         pl.semaphore_signal(barrier, inc=1, device_id=partner, device_id_type=MESH)
 
@@ -233,7 +221,7 @@
                 for i, at in enumerate(ats):
                     xs[s, lc, d, at, :] = res[d * CAP : (d + 1) * CAP, i * COLS : (i + 1) * COLS]
 
-    def accumulate(s, lc, h, dst):
+    def accumulate(s, lc, h, dst, place):
         for ats, layer in pairs(lc, h):
             cols = [
                 jnp.concatenate(
@@ -243,7 +231,7 @@
             ]
             res = jnp.dot(total[s], jnp.concatenate(cols, axis=1), preferred_element_type=F32)
             for i in range(2):
-                dst[pl.ds((layer + i) * BLOCKS, BLOCKS), :] = res[:, i * COLS : (i + 1) * COLS]
+                dst[place(layer + i), :] = res[:, i * COLS : (i + 1) * COLS]
 
     first = STEPS - 1
     tail = (LAYERS - 1) * BLOCKS
@@ -274,7 +262,7 @@
             def load(b):
                 return fs[pl.ds(b, LAYERS, stride=BLOCKS), :]
 
-        a1, a2, x, via = {}, {}, {}, {}
+        a1, a2, x = {}, {}, {}
 
         def send_adjoint(lc, k):
             a1[lc, k] = send(
@@ -297,39 +285,28 @@
                     a2_s.at[s, lc, h, k - 1], a2_r.at[s, lc, h, k - 1], over_y(CLS - k),
                 )
 
-        def send_along(lc, h, d, src, device):
-            x[lc, h, d] = send(
-                src, xr.at[s, lc, d - 1, rows(h)],
-                x_s.at[s, lc, h, d - 1], x_r.at[s, lc, h, d - 1], device,
-            )
-
         def depart(lc, h):
             for k in range(1, CLS):
                 a2[lc, h, k].wait_recv()
             pack(s, lc, h)
-            far = xs.at[s, lc, REACH - 1, rows(h)]
-            if (lc, h) in DIRECT:
-                send_along(lc, h, REACH, far, along(-REACH))
-            else:
-                via[lc, h] = send(
-                    far, rl.at[s, lc, rows(h)], rl_s.at[s, lc, h], rl_r.at[s, lc, h], relay
-                )
-            for d in range(REACH - 1, 0, -1):
-                send_along(lc, h, d, xs.at[s, lc, d - 1, rows(h)], along(-d))
-
-        def forward(lc, h):
-            if (lc, h) not in DIRECT:
-                via[lc, h].wait_recv()
-                send_along(lc, h, REACH, rl.at[s, lc, rows(h)], final)
+            for d in range(REACH, 0, -1):
+                x[lc, h, d] = send(
+                    xs.at[s, lc, d - 1, rows(h)], xr.at[s, lc, d - 1, rows(h)],
+                    x_s.at[s, lc, h, d - 1], x_r.at[s, lc, h, d - 1], along(-d),
+                )
 
         def arrive(lc, h):
             for d in range(1, REACH + 1):
                 x[lc, h, d].wait_recv()
-            accumulate(s, lc, h, fs)
-            if s == 0:
-                size = HALF // OWN * BLOCKS
-                at = pl.ds((lc * 2 + h) * size, size)
-                copy = pltpu.make_async_copy(fs.at[at, :], out.at[at, :], out_sem.at[lc, h])
+            if s > 0:
+                accumulate(s, lc, h, fs, lambda layer: pl.ds(layer * BLOCKS, BLOCKS))
+                return
+            accumulate(s, lc, h, ob, lambda layer: pl.ds(layer, BLOCKS, stride=LAYERS))
+            if h == 1:
+                at = pl.ds(lc * CHUNK, CHUNK)
+                copy = pltpu.make_async_copy(
+                    ob.reshape(BLOCKS, LAYERS, COLS).at[:, at, :], out.at[:, at, :], out_sem.at[lc]
+                )
                 copy.start()
                 stores.append(copy)
 
@@ -355,32 +332,44 @@
         send_back(c1, 1)
         depart(c0, 0)
         depart(c0, 1)
-        forward(c0, 0)
         depart(c1, 0)
-        forward(c0, 1)
         exchange(c2)
         send_back(c2, 0)
         send_back(c2, 1)
         depart(c1, 1)
-        forward(c1, 0)
         arrive(c0, 0)
         arrive(c0, 1)
         depart(c2, 0)
-        forward(c1, 1)
         depart(c2, 1)
         if s > 0:
             bed_out[s - 1] = my_rate * fs[pl.ds(tail, BLOCKS), :]
             beds = send_bed(s - 1)
-        forward(c2, 0)
         arrive(c1, 0)
         arrive(c1, 1)
-        forward(c2, 1)
         arrive(c2, 0)
         arrive(c2, 1)
 
     for copy in pending:
         copy.wait_send()
     for copy in stores:
+        copy.wait()
+
+
+def place_result(src, dst, held, in_sem, out_sem):
+    size = BLOCKS // PIECES
+    pieces = [pl.ds(i * size, size) for i in range(PIECES)]
+    ins = [
+        pltpu.make_async_copy(src.at[at], held.at[at], in_sem.at[i]) for i, at in enumerate(pieces)
+    ]
+    outs = [
+        pltpu.make_async_copy(held.at[at], dst.at[at], out_sem.at[i]) for i, at in enumerate(pieces)
+    ]
+    for copy in ins:
+        copy.start()
+    for into, onward in zip(ins, outs):
+        into.wait()
+        onward.start()
+    for copy in outs:
         copy.wait()
 
 
@@ -389,7 +378,7 @@
     dma = pltpu.SemaphoreType.DMA
     result = pl.pallas_call(
         kernel,
-        out_shape=jax.ShapeDtypeStruct((LAYERS * BLOCKS, COLS), F32),
+        out_shape=jax.ShapeDtypeStruct((BLOCKS, LAYERS, COLS), F32),
         in_specs=[hbm] * 5 + [pl.BlockSpec(memory_space=pltpu.SMEM)],
         out_specs=hbm,
         scratch_shapes=[
@@ -404,7 +393,7 @@
             pltpu.VMEM((STEPS, CHUNKS, CLS, ROWS, COLS), BF16),
             pltpu.VMEM((STEPS, CHUNKS, REACH, ROWS, COLS), BF16),
             pltpu.VMEM((STEPS, CHUNKS, REACH, ROWS, COLS), BF16),
-            pltpu.VMEM((STEPS, CHUNKS, ROWS, COLS), BF16),
+            pltpu.VMEM((LAYERS * BLOCKS, COLS), F32),
             pltpu.VMEM((LAYERS * BLOCKS, COLS), F32),
             pltpu.VMEM((CLS, ROWS, COLS), F32),
             pltpu.VMEM((STEPS, BLOCKS, COLS), F32),
@@ -414,19 +403,25 @@
             pltpu.VMEM((STEPS, BLOCKS, BLOCKS), BF16),
             pltpu.VMEM((STEPS, BLOCKS, 2 * BLOCKS), BF16),
             dma((6,)),
-            dma((CHUNKS, 2)),
+            dma((CHUNKS,)),
         ]
         + [dma((STEPS, CLS, CLS - 1))] * 2
         + [dma((STEPS, CHUNKS, CLS - 1))] * 2
         + [dma((STEPS, CHUNKS, 2, CLS - 1))] * 2
-        + [dma((STEPS, CHUNKS, 2, REACH))] * 2
-        + [dma((STEPS, CHUNKS, 2))] * 2,
+        + [dma((STEPS, CHUNKS, 2, REACH))] * 2,
         compiler_params=pltpu.CompilerParams(
             collective_id=0, has_side_effects=True, vmem_limit_bytes=56 * 1024 * 1024
         ),
         cost_estimate=pl.CostEstimate(flops=2_000_000_000, bytes_accessed=6_000_000, transcendentals=0),
     )(cotangent[0], departure, interp, vertical_inv, regime, bed_rate)
-    return jnp.swapaxes(result.reshape(LAYERS, BLOCKS, COLS), 0, 1)[None]
+    return pl.pallas_call(
+        place_result,
+        out_shape=jax.ShapeDtypeStruct((BLOCKS, LAYERS, COLS), F32),
+        in_specs=[hbm],
+        out_specs=hbm,
+        scratch_shapes=[pltpu.VMEM((BLOCKS, LAYERS, COLS), F32), dma((PIECES,)), dma((PIECES,))],
+        compiler_params=pltpu.CompilerParams(vmem_limit_bytes=56 * 1024 * 1024),
+    )(result)[None]
 
 
 def solution(mesh):

time: 75.4 us -> 72.5 us (0.962)
  local copies, waits for them, and re-layouts: 3.46 us -> 0 us
  Pallas kernels: 71 us -> 72.3 us
    reshape x1 -> x0, local copies, waits for them, and re-layouts: 3.46 us -> none  [local(): return jnp.swapaxes(result.reshape(LAYERS, BLOCKS, COLS), 0, 1)[None]]
    pallas_call x1 -> x2, Pallas kernels: 71 us -> 72.3 us  [the longest x1 70.1 us: local(): pl.pallas_call(kernel, out_shape=jax.ShapeDtypeStruct((BLOCKS, LAYERS, CO...]
where the time goes in v3:
time: 72.5 us; the launch traced here: 72.3 us
  Pallas kernels  72.3 us (100%)
    pallas_call x1, Pallas kernels, local(): pl.pallas_call(kernel, out_shape=jax.ShapeDtypeStruct((BLOCKS, LAYERS, CO...  70.1 us
    pallas_call x1, Pallas kernels, local(): pl.pallas_call(place_result, out_shape=jax.ShapeDtypeStruct((BLOCKS, LAYE...  2.2 us

profile of v3, /device:TPU:71, one launch (start us, length us, event | category | flops | bytes accessed | tf_op | source)
XLA Modules:
  0.0 72.3 jit_solution(16184890665155463079)
XLA Ops:
  0.0 70.1 %shard_map.64.src = f32[128,24,128]{2,1,0:T(8,128)} custom-call(f32[128,24,128]{2,1,0:T(8,128)} %bitcast.2, s32[2,8192]{1,0:T(2,128)} %dep_hbm.1, bf16[2,32,128,128]{3,2,1,0:T(8,128)(2,1)} %w_hbm.1, f32[4,4,24,24]{3,2,1,0:T(8,128)} %v_hbm.1, s32[128,128]{1,0:T(8,128)} %reg_hbm.1, f32[4]{0:T(128)} %rate.1), custom_call_target="tpu_custom_call" | custom-call | flops 2000000000 | bytes 6000000 | tf_op jit(solution)/shard_map/pallas_call | solution.py:379
  70.1 2.2 %shard_map.65 = f32[128,24,128]{2,1,0:T(8,128)} custom-call(f32[128,24,128]{2,1,0:T(8,128)} %shard_map.64.src), custom_call_target="tpu_custom_call" | custom-call | tf_op jit(solution)/shard_map/pallas_call | solution.py:417

commit v4 on v3

--- a/solution.py
+++ b/solution.py
@@ -21,6 +21,8 @@
 DESTS = (2, 1, 3, 0)
 PIECES = 4
 ROWS = CHUNK * OWN
+STEP = OWN + 8
+PITCH = BLOCKS + 8
 HALF = ROWS // 2
 V_PAIRS = 16
 I_PAIRS = 16
@@ -196,14 +198,16 @@
                 )
             for n, x in zip(ns, res):
                 for k in range(CLS):
-                    pf[k, pl.ds(2 * n, CHUNK, stride=OWN), :] = x[k * 16 : k * 16 + 8, :COLS]
-                    pf[k, pl.ds(2 * n + 1, CHUNK, stride=OWN), :] = x[k * 16 + 8 : k * 16 + 16, COLS:]
+                    pf[k, pl.ds(2 * n, CHUNK, stride=STEP), :] = x[k * 16 : k * 16 + 8, :COLS]
+                    pf[k, pl.ds(2 * n + 1, CHUNK, stride=STEP), :] = x[k * 16 + 8 : k * 16 + 16, COLS:]
             return carry
 
         lax.fori_loop(0, OWN // 2 // I_PAIRS, body, 0)
-        for k in range(1, CLS):
-            sb[s, lc, k - 1] = pf[k].astype(BF16)
-        pr[s, lc, cls] = pf[0].astype(BF16)
+        for i in range(CHUNK):
+            at, packed = pl.ds(i * STEP, OWN), pl.ds(i * OWN, OWN)
+            for k in range(1, CLS):
+                sb[s, lc, k - 1, packed, :] = pf[k, at, :].astype(BF16)
+            pr[s, lc, cls, packed, :] = pf[0, at, :].astype(BF16)
 
     def plane_of(s, lc, at):
         return jnp.concatenate([pr[s, lc, y, at, :] for y in range(CLS)], axis=0)
@@ -234,7 +238,7 @@
                 dst[place(layer + i), :] = res[:, i * COLS : (i + 1) * COLS]
 
     first = STEPS - 1
-    tail = (LAYERS - 1) * BLOCKS
+    tail = (LAYERS - 1) * PITCH
     loads[0].wait()
     bed_out[first] = my_rate * cot[:, LAYERS - 1, :]
     pl.semaphore_wait(barrier, len(partners))
@@ -242,6 +246,8 @@
     for copy in loads[1:]:
         copy.wait()
     build_operators(v_ref, lhs, cls)
+    for s in range(STEPS):
+        build_tables(dep, gather, total, s, me)
 
     stores = []
     for s in range(STEPS - 1, -1, -1):
@@ -256,11 +262,11 @@
         else:
 
             def add_bottom(i, dest):
-                at = pl.ds(pl.multiple_of(tail + dest * OWN, OWN), OWN)
+                at = pl.ds(pl.multiple_of(tail + dest * OWN, 8), OWN)
                 fs[at, :] = fs[at, :] + bottom_of(s, beds, i, dest)
 
             def load(b):
-                return fs[pl.ds(b, LAYERS, stride=BLOCKS), :]
+                return fs[pl.ds(b, LAYERS, stride=PITCH), :]
 
         a1, a2, x = {}, {}, {}
 
@@ -299,7 +305,7 @@
             for d in range(1, REACH + 1):
                 x[lc, h, d].wait_recv()
             if s > 0:
-                accumulate(s, lc, h, fs, lambda layer: pl.ds(layer * BLOCKS, BLOCKS))
+                accumulate(s, lc, h, fs, lambda layer: pl.ds(layer * PITCH, BLOCKS))
                 return
             accumulate(s, lc, h, ob, lambda layer: pl.ds(layer, BLOCKS, stride=LAYERS))
             if h == 1:
@@ -319,9 +325,6 @@
                 send_adjoint(c0, i)
         for k in DESTS[:-1]:
             send_adjoint(c1, k)
-        if s == first:
-            for each in range(STEPS - 1, -1, -1):
-                build_tables(dep, gather, total, each, me)
         exchange(c0)
         send_back(c0, 0)
         send_back(c0, 1)
@@ -339,11 +342,11 @@
         depart(c1, 1)
         arrive(c0, 0)
         arrive(c0, 1)
-        depart(c2, 0)
-        depart(c2, 1)
         if s > 0:
             bed_out[s - 1] = my_rate * fs[pl.ds(tail, BLOCKS), :]
             beds = send_bed(s - 1)
+        depart(c2, 0)
+        depart(c2, 1)
         arrive(c1, 0)
         arrive(c1, 1)
         arrive(c2, 0)
@@ -393,9 +396,9 @@
             pltpu.VMEM((STEPS, CHUNKS, CLS, ROWS, COLS), BF16),
             pltpu.VMEM((STEPS, CHUNKS, REACH, ROWS, COLS), BF16),
             pltpu.VMEM((STEPS, CHUNKS, REACH, ROWS, COLS), BF16),
+            pltpu.VMEM((LAYERS * PITCH, COLS), F32),
             pltpu.VMEM((LAYERS * BLOCKS, COLS), F32),
-            pltpu.VMEM((LAYERS * BLOCKS, COLS), F32),
-            pltpu.VMEM((CLS, ROWS, COLS), F32),
+            pltpu.VMEM((CLS, CHUNK * STEP, COLS), F32),
             pltpu.VMEM((STEPS, BLOCKS, COLS), F32),
             pltpu.VMEM((STEPS, CLS - 1, BLOCKS, COLS), F32),
             pltpu.VMEM((BLOCKS, COLS), F32),

time: 72.5 us -> 71.4 us (0.985)
  Pallas kernels: 72.3 us -> 71.3 us
    pallas_call x1, Pallas kernels: 70.1 us -> 69.1 us  [local(): pl.pallas_call(kernel, out_shape=jax.ShapeDtypeStruct((BLOCKS, LAYERS, CO...]
where the time goes in v4:
time: 71.4 us; the launch traced here: 71.3 us
  Pallas kernels  71.3 us (100%)
    pallas_call x1, Pallas kernels, local(): pl.pallas_call(kernel, out_shape=jax.ShapeDtypeStruct((BLOCKS, LAYERS, CO...  69.1 us
    pallas_call x1, Pallas kernels, local(): pl.pallas_call(place_result, out_shape=jax.ShapeDtypeStruct((BLOCKS, LAYE...  2.2 us

profile of v4, /device:TPU:71, one launch (start us, length us, event | category | flops | bytes accessed | tf_op | source)
XLA Modules:
  0.0 71.3 jit_solution(2866151729906844440)
XLA Ops:
  0.0 69.1 %shard_map.64.src = f32[128,24,128]{2,1,0:T(8,128)} custom-call(f32[128,24,128]{2,1,0:T(8,128)} %bitcast.2, s32[2,8192]{1,0:T(2,128)} %dep_hbm.1, bf16[2,32,128,128]{3,2,1,0:T(8,128)(2,1)} %w_hbm.1, f32[4,4,24,24]{3,2,1,0:T(8,128)} %v_hbm.1, s32[128,128]{1,0:T(8,128)} %reg_hbm.1, f32[4]{0:T(128)} %rate.1), custom_call_target="tpu_custom_call" | custom-call | flops 2000000000 | bytes 6000000 | tf_op jit(solution)/shard_map/pallas_call | solution.py:382
  69.1 2.2 %shard_map.65 = f32[128,24,128]{2,1,0:T(8,128)} custom-call(f32[128,24,128]{2,1,0:T(8,128)} %shard_map.64.src), custom_call_target="tpu_custom_call" | custom-call | tf_op jit(solution)/shard_map/pallas_call | solution.py:420

commit v5 on v4

--- a/solution.py
+++ b/solution.py
@@ -141,7 +141,7 @@
     def send_bed(s):
         copies = {}
         for i in DESTS:
-            for k in range(1, CLS):
+            for k in DESTS[:-1]:
                 at = own_rows(lax.rem(cls + k + i, CLS))
                 copies[i, k] = send(
                     bed_out.at[s, at], bed_in.at[s, k - 1, at],
@@ -340,12 +340,12 @@
         send_back(c2, 0)
         send_back(c2, 1)
         depart(c1, 1)
+        depart(c2, 0)
         arrive(c0, 0)
         arrive(c0, 1)
         if s > 0:
             bed_out[s - 1] = my_rate * fs[pl.ds(tail, BLOCKS), :]
             beds = send_bed(s - 1)
-        depart(c2, 0)
         depart(c2, 1)
         arrive(c1, 0)
         arrive(c1, 1)

time: 71.4 us -> 71 us (level); the launches traced: 71.3 us -> 70.1 us
  Pallas kernels: 71.3 us -> 70.1 us
    pallas_call x1, Pallas kernels: 69.1 us -> 67.9 us  [local(): pl.pallas_call(kernel, out_shape=jax.ShapeDtypeStruct((BLOCKS, LAYERS, CO...]
where the time goes in v5:
time: 71 us; the launch traced here: 70.1 us
  Pallas kernels  70.1 us (99%)
    pallas_call x1, Pallas kernels, local(): pl.pallas_call(kernel, out_shape=jax.ShapeDtypeStruct((BLOCKS, LAYERS, CO...  67.9 us
    pallas_call x1, Pallas kernels, local(): pl.pallas_call(place_result, out_shape=jax.ShapeDtypeStruct((BLOCKS, LAYE...  2.2 us

profile of v5, /device:TPU:71, one launch (start us, length us, event | category | flops | bytes accessed | tf_op | source)
XLA Modules:
  0.0 70.1 jit_solution(2844771438701907302)
XLA Ops:
  0.0 67.9 %shard_map.64.src = f32[128,24,128]{2,1,0:T(8,128)} custom-call(f32[128,24,128]{2,1,0:T(8,128)} %bitcast.2, s32[2,8192]{1,0:T(2,128)} %dep_hbm.1, bf16[2,32,128,128]{3,2,1,0:T(8,128)(2,1)} %w_hbm.1, f32[4,4,24,24]{3,2,1,0:T(8,128)} %v_hbm.1, s32[128,128]{1,0:T(8,128)} %reg_hbm.1, f32[4]{0:T(128)} %rate.1), custom_call_target="tpu_custom_call" | custom-call | flops 2000000000 | bytes 6000000 | tf_op jit(solution)/shard_map/pallas_call | solution.py:382
  67.9 2.2 %shard_map.65 = f32[128,24,128]{2,1,0:T(8,128)} custom-call(f32[128,24,128]{2,1,0:T(8,128)} %shard_map.64.src), custom_call_target="tpu_custom_call" | custom-call | tf_op jit(solution)/shard_map/pallas_call | solution.py:420
